TPU v7x, 32 devices: a whole 2x2x4 slice. The times are simulated.
32 devices in a mesh: dom: 8 (over z, x), cls: 4 (over y, core).
Axes of the slice: x: 2, y: 2, z: 4, core: 2. Of those that a mesh axis runs over, the one named last changes fastest.
Arguments:
- particles: bfloat16 [256, 16384], P(('dom', 'cls')), may hold values from -6 to 6
- references: bfloat16 [64, 16384], P('cls'), may hold values from -0.046875 to 0.046875
- pose_weights: int32 [256, 24, 64], P(('dom', 'cls')), may hold values from 0 to 4
- class_mask: int32 [256, 64], P(('dom', 'cls')), may hold values 0 or 1
Outputs:
- class_scores: float32 [256, 64], P(('dom', 'cls'))
- class_sums: float32 [64, 16384], P('cls', 'dom')
All inputs are finite; a program needn't handle non-finite values. No bound on the sum of `class_mask` on one device may be relied on, other than what follows from the above.
Results may differ from a plain program's by a relative error of at most 0.0003.
Values may be sent and summed in bfloat16 or wider, within the bound.
No kernel may reach another device: no remote copies, remote signals or barrier semaphores. Data moves between devices by JAX's collectives and lax.ppermute only.
A program may use at most 128 MiB of HBM per device.

v0:
```python
import math
import jax
import jax.numpy as jnp
from jax import lax
from jax.sharding import PartitionSpec as P

CYCLES = 64
ANG = 256
ROT = 24


def turned(images, shift_by):
    shape_in = images.shape
    polar = images.reshape(shape_in[:-1] + (CYCLES, ANG))
    return jnp.roll(polar, shift_by, axis=-1).reshape(shape_in)


def on_device(particles, references, pose_weights, class_mask):
    n_rows = particles.shape[0]
    angle_step = ANG // ROT
    weights = pose_weights * class_mask[:, None, :]
    weights_f = weights.astype(jnp.float32)
    weights_b = weights.astype(jnp.bfloat16)
    rotated = jnp.stack([turned(particles, -r * angle_step) for r in range(ROT)], axis=0)
    rotated_rows = rotated.reshape(ROT * n_rows, rotated.shape[2])
    ref_piece = lax.all_gather(references, "cls", axis=0, tiled=True)
    width_now = ref_piece.shape[0]
    corr = jnp.dot(rotated_rows, ref_piece.T, preferred_element_type=jnp.float32)
    corr = corr.reshape(ROT, n_rows, width_now)
    weight_cols = weights_f
    scored = jnp.einsum("rnk,nrk->nk", corr, weight_cols) / ROT
    weight_cols = weights_b
    local_sums = lax.psum_scatter(
        jnp.einsum("nrk,rnl->kl", weight_cols, rotated, preferred_element_type=jnp.float32),
        "cls",
        scatter_dimension=0,
        tiled=True,
    )
    home_part = lax.psum_scatter(local_sums, "dom", scatter_dimension=1, tiled=True)
    particle_total = n_rows * lax.axis_size("dom") * lax.axis_size("cls")
    class_sums = home_part / math.sqrt(particle_total * ROT)
    return (scored, class_sums)


def solution(mesh):
    return jax.shard_map(
        on_device,
        mesh=mesh,
        in_specs=(
            P(("dom", "cls"), None),
            P("cls", None),
            P(("dom", "cls"), None, None),
            P(("dom", "cls"), None),
        ),
        out_specs=(P(("dom", "cls"), None), P("cls", "dom")),
        check_vma=False,
    )
```

profile of v0, /device:TPU:0, one launch (start us, length us, event | category | flops | bytes accessed | tf_op | source)
XLA Modules:
  0.0 300.9 jit_solution(10851470049415356779)
XLA Ops:
  20.6 1.8 slice.250
  24.0 1.8 slice.252
  49.3 1.8 stack_reshape.106
  53.8 1.8 stack_reshape.107
  58.3 1.7 stack_reshape.96
  62.8 1.8 stack_reshape.97
  67.3 1.8 stack_reshape.98
  71.8 1.8 stack_reshape.99
  75.4 1.7 stack_reshape.108
  79.0 1.7 stack_reshape.109
  82.6 1.8 stack_reshape.110
  86.2 1.8 stack_reshape.111
  89.7 1.7 stack_reshape.112
  93.3 1.7 stack_reshape.113
  96.9 1.8 stack_reshape.114
  100.5 1.8 stack_reshape.115
  104.1 1.7 stack_reshape.116
  110.3 1.8 stack_reshape.118
  113.3 34.4 %stack.3 = bf16[24,8,16384]{2,0,1:T(8,128)(2,1)} concatenate(bf16[1,8,16384]{2,0,1:T(2,128)(2,1)} %copy.98, bf16[1,8,16384]{2,0,1:T(2,128)(2,1)} %stack_reshape.96, bf16[1,8,16384]{2,0,1:T(2,128)(2,1)} %stack_reshape.97, bf16[1,8,16384]{2,0,1:T(2,128)(2,1)} %stack_reshape.98, bf16[1,8,16384]{2,0,1:T(2,128)(2,1)} %stack_reshape.99, bf16[1,8,16384]{2,0,1:T(2,128)(2,1)S(1)} %stack_reshape.100, ...), dimensions={0} | concatenate | bytes 12582912 | tf_op jit(solution)/shard_map/stack | solution.py:24
  147.7 6.2 %convolution_bitcast_fusion = f32[64,16384]{1,0:T(8,128)} fusion(bf16[24,8,16384]{2,0,1:T(8,128)(2,1)} %stack.3, s32[8,24,64]{2,1,0:T(8,128)S(1)} %copy-done.2, s32[8,64]{1,0:T(8,128)S(1)} %copy-done.1), kind=kOutput, calls=%fused_computation | convolution fusion | flops 402677760 | bytes 10536960 | tf_op jit(solution)/shard_map/nrk,rnl->kl/dot_general | solution.py:34
  154.7 46.6 %reduce-scatter.3.cloned.1.call-done = f32[16,16384]{1,0:T(8,128)} async-done(((f32[64,16384]{1,0:T(8,128)}), f32[16,16384]{1,0:T(8,128)}) %reduce-scatter.3.cloned.1.call-update) | async-done | bytes 1048592 | tf_op jit(solution)/shard_map/reduce_scatter | solution.py:33
  201.3 24.2 %all-gather.2.cloned.1.call-done = bf16[64,16384]{1,0:T(8,128)(2,1)} async-done(((bf16[16,16384]{1,0:T(8,128)(2,1)}), bf16[64,16384]{1,0:T(8,128)(2,1)}) %all-gather.2.cloned.1.call-update) | async-done | bytes 2097168 | tf_op jit(solution)/shard_map/all_gather | solution.py:26
  225.5 5.2 %fusion.8 = f32[8,64]{1,0:T(8,128)S(1)} fusion(bf16[24,8,16384]{2,0,1:T(8,128)(2,1)} %stack.3, bf16[64,16384]{1,0:T(8,128)(2,1)} %all-gather.2.cloned.1.call-done, s32[8,24,64]{2,1,0:T(8,128)S(1)} %copy-done.2, s32[8,64]{1,0:T(8,128)S(1)} %copy-done.1), kind=kOutput, calls=%fused_computation.5 | convolution fusion | flops 402701824 | bytes 8441856 | tf_op jit(solution)/shard_map/dot_general | solution.py:28
  231.3 61.4 %reduce-scatter.5.cloned.1.call-done = f32[16,2048]{1,0:T(8,128)} async-done(((f32[16,16384]{1,0:T(8,128)}), f32[16,2048]{1,0:T(8,128)}) %reduce-scatter.5.cloned.1.call-update) | async-done | bytes 131088 | tf_op jit(solution)/shard_map/reduce_scatter | solution.py:39
  (124 shorter events, 76.9 us)
Async XLA Ops:
  7.2 20.2 %copy-start = (bf16[8,16384]{1,0:T(8,128)(2,1)S(1)}, bf16[8,16384]{1,0:T(8,128)(2,1)}, u32[]{:S(2)}) copy-start(bf16[8,16384]{1,0:T(8,128)(2,1)} %param.4) | copy-start | bytes 786436
  7.2 194.1 %reduce-scatter.3.cloned.1.call-start = ((), (), s32[]{:S(2)}) async-start(), calls=%async_computation.3 | async-start | bytes 5242880 | tf_op jit(solution)/shard_map/reduce_scatter | solution.py:33
  113.3 34.4 %copy-start.1 = (s32[8,64]{1,0:T(8,128)S(1)}, s32[8,64]{1,0:T(8,128)}, u32[]{:S(2)}) copy-start(s32[8,64]{1,0:T(8,128)} %param.7) | copy-start | bytes 6148
  113.3 34.4 %copy-start.2 = (s32[8,24,64]{2,1,0:T(8,128)S(1)}, s32[8,24,64]{2,1,0:T(8,128)}, u32[]{:S(2)}) copy-start(s32[8,24,64]{2,1,0:T(8,128)} %param.6) | copy-start | bytes 147460
  153.9 71.6 %all-gather.2.cloned.1.call-start = ((), (), s32[]{:S(2)}) async-start(), calls=%async_computation.2 | async-start | bytes 2621440 | tf_op jit(solution)/shard_map/all_gather | solution.py:26
  154.6 138.1 %reduce-scatter.5.cloned.1.call-start = ((), (), s32[]{:S(2)}) async-start(), calls=%async_computation.4 | async-start | bytes 1179648 | tf_op jit(solution)/shard_map/reduce_scatter | solution.py:39
Sparse Core Ops, SparseCore 0:
  154.0 47.2 reduce-scatter.2
  202.9 22.5 all-gather.1
  229.3 63.4 reduce-scatter.4
where the time goes:
time: 306 us; the launch traced here: 301 us
  waiting for transfers between devices  133 us (43%)
  local copies, waits for them, and re-layouts  125 us (41%)
  other arithmetic  17.7 us (6%)
  between operations  14.2 us (5%)
  matrix products  11.4 us (4%)
    another operation x25, local copies, waits for them, and re-layouts, on_device(): jnp.stack([turned(particles, -r * angle_step) for r in range(ROT)], axis=0)  67.3 us
    reduce_scatter x1, waiting for transfers between devices, on_device(): lax.psum_scatter(local_sums, 'dom', scatter_dimension=1, tiled=True)  61.4 us
    reduce_scatter x1, waiting for transfers between devices, on_device(): lax.psum_scatter(jnp.einsum('nrk,rnl->kl', weight_cols, rotated, preferre...  46.6 us
    slice x35, local copies, waits for them, and re-layouts, turned(): return jnp.roll(polar, shift_by, axis=-1).reshape(shape_in)  33.7 us
    all_gather x1, waiting for transfers between devices, on_device(): ref_piece = lax.all_gather(references, 'cls', axis=0, tiled=True)  24.2 us
    unnamed x52, local copies, waits for them, and re-layouts  23.6 us
    concatenate x23, other arithmetic, turned(): return jnp.roll(polar, shift_by, axis=-1).reshape(shape_in)  15.5 us
    dot_general x1, matrix products, on_device(): jnp.einsum('nrk,rnl->kl', weight_cols, rotated, preferred_element_type=jn...  6.15 us
  transfers between devices with their start and end apart: 3, of which 3 were waited for; matrix products, arithmetic and copies ran while one was open for 2% of the time, Pallas kernels for 0%

commit v1 on v0

--- a/solution.py
+++ b/solution.py
@@ -7,6 +7,23 @@
 CYCLES = 64
 ANG = 256
 ROT = 24
+
+
+def joined_along(pieces, dim):
+    pieces = jnp.moveaxis(pieces, 0, dim)
+    lengths = pieces.shape
+    return pieces.reshape(*lengths[:dim], lengths[dim] * lengths[dim + 1], *lengths[dim + 2 :])
+
+
+def collected_by_bits(shard, axis):
+    size, place = (lax.axis_size(axis), lax.axis_index(axis))
+    blocks, distance = (shard[None], 1)
+    while distance < size:
+        theirs = lax.ppermute(blocks, axis, [(i, i ^ distance) for i in range(size)])
+        low = place & distance == 0
+        blocks = jnp.concatenate([jnp.where(low, blocks, theirs), jnp.where(low, theirs, blocks)])
+        distance *= 2
+    return blocks
 
 
 def turned(images, shift_by):
@@ -23,7 +40,7 @@
     weights_b = weights.astype(jnp.bfloat16)
     rotated = jnp.stack([turned(particles, -r * angle_step) for r in range(ROT)], axis=0)
     rotated_rows = rotated.reshape(ROT * n_rows, rotated.shape[2])
-    ref_piece = lax.all_gather(references, "cls", axis=0, tiled=True)
+    ref_piece = joined_along(collected_by_bits(references, "cls"), 0)
     width_now = ref_piece.shape[0]
     corr = jnp.dot(rotated_rows, ref_piece.T, preferred_element_type=jnp.float32)
     corr = corr.reshape(ROT, n_rows, width_now)

time: 306 us -> 285 us (0.931)
  waiting for transfers between devices: 133 us -> 110 us
  local copies, waits for them, and re-layouts: 125 us -> 121 us
  starting transfers between devices: 0.12 us -> 3.38 us
    reduce_scatter x1, waiting for transfers between devices: 46.6 us -> 16 us  [on_device(): lax.psum_scatter(jnp.einsum('nrk,rnl->kl', weight_cols, rotated, preferre...]
    ppermute x0 -> x2, waiting for transfers between devices: none -> 30.3 us  [collected_by_bits(): lax.ppermute(blocks, axis, [(i, i ^ distance) for i in range(size)])]
    all_gather x1 -> x0, waiting for transfers between devices: 24.2 us -> none  [on_device(): ref_piece = lax.all_gather(references, 'cls', axis=0, tiled=True)]
    slice x35, local copies, waits for them, and re-layouts: 33.7 us -> 29.2 us  [turned(): return jnp.roll(polar, shift_by, axis=-1).reshape(shape_in)]
    ppermute x0 -> x2, starting transfers between devices: none -> 3.12 us  [collected_by_bits(): lax.ppermute(blocks, axis, [(i, i ^ distance) for i in range(size)])]
    unnamed x52 -> x54, local copies, waits for them, and re-layouts: 23.6 us -> 24.3 us
  transfers between devices with their start and end apart: 3 -> 4, of which waited for: 3 -> 3; matrix products, arithmetic and copies ran while one was open for 2% -> 54% of each run, Pallas kernels for 0% -> 0%
where the time goes in v1:
time: 285 us; the launch traced here: 280 us
  local copies, waits for them, and re-layouts  121 us (42%)
  waiting for transfers between devices  110 us (39%)
  other arithmetic  20.6 us (7%)
  between operations  14.5 us (5%)
  matrix products  10.8 us (4%)
  starting transfers between devices  3.38 us (1%)
    another operation x25, local copies, waits for them, and re-layouts, on_device(): jnp.stack([turned(particles, -r * angle_step) for r in range(ROT)], axis=0)  67.2 us
    reduce_scatter x1, waiting for transfers between devices, on_device(): lax.psum_scatter(local_sums, 'dom', scatter_dimension=1, tiled=True)  63.3 us
    ppermute x2, waiting for transfers between devices, collected_by_bits(): lax.ppermute(blocks, axis, [(i, i ^ distance) for i in range(size)])  30.3 us
    slice x35, local copies, waits for them, and re-layouts, turned(): return jnp.roll(polar, shift_by, axis=-1).reshape(shape_in)  29.2 us
    unnamed x54, local copies, waits for them, and re-layouts  24.3 us
    reduce_scatter x1, waiting for transfers between devices, on_device(): lax.psum_scatter(jnp.einsum('nrk,rnl->kl', weight_cols, rotated, preferre...  16 us
    concatenate x23, other arithmetic, turned(): return jnp.roll(polar, shift_by, axis=-1).reshape(shape_in)  15.6 us
    dot_general x1, matrix products, on_device(): jnp.einsum('nrk,rnl->kl', weight_cols, rotated, preferred_element_type=jn...  6.16 us
  transfers between devices with their start and end apart: 4, of which 3 were waited for; matrix products, arithmetic and copies ran while one was open for 54% of the time, Pallas kernels for 0%

profile of v1, /device:TPU:0, one launch (start us, length us, event | category | flops | bytes accessed | tf_op | source)
XLA Modules:
  0.0 279.7 jit_solution(933967110644012055)
XLA Ops:
  45.3 1.8 stack_reshape.106
  49.8 1.8 stack_reshape.107
  54.3 1.7 stack_reshape.96
  58.7 1.8 stack_reshape.97
  63.3 1.8 stack_reshape.98
  67.8 1.8 stack_reshape.99
  71.5 1.7 stack_reshape.108
  75.0 1.7 stack_reshape.109
  78.6 1.8 stack_reshape.110
  82.2 1.8 stack_reshape.111
  85.8 1.8 stack_reshape.112
  89.4 1.8 stack_reshape.113
  93.0 1.8 stack_reshape.114
  96.6 1.7 stack_reshape.115
  100.2 1.7 stack_reshape.116
  103.8 1.8 stack_reshape.117
  106.5 1.8 stack_reshape.118
  109.4 34.4 %stack.3 = bf16[24,8,16384]{2,0,1:T(8,128)(2,1)} concatenate(bf16[1,8,16384]{2,0,1:T(2,128)(2,1)} %copy.98, bf16[1,8,16384]{2,0,1:T(2,128)(2,1)} %stack_reshape.96, bf16[1,8,16384]{2,0,1:T(2,128)(2,1)} %stack_reshape.97, bf16[1,8,16384]{2,0,1:T(2,128)(2,1)} %stack_reshape.98, bf16[1,8,16384]{2,0,1:T(2,128)(2,1)} %stack_reshape.99, bf16[1,8,16384]{2,0,1:T(2,128)(2,1)S(1)} %stack_reshape.100, ...), dimensions={0} | concatenate | bytes 12582912 | tf_op jit(solution)/shard_map/stack | solution.py:41
  143.8 6.2 %convolution_bitcast_fusion = f32[64,16384]{1,0:T(8,128)} fusion(bf16[24,8,16384]{2,0,1:T(8,128)(2,1)} %stack.3, s32[8,24,64]{2,1,0:T(8,128)S(1)} %copy-done.3, s32[8,64]{1,0:T(8,128)S(1)} %copy-done.2), kind=kOutput, calls=%fused_computation | convolution fusion | flops 402677760 | bytes 10536960 | tf_op jit(solution)/shard_map/nrk,rnl->kl/dot_general | solution.py:51
  152.2 2.6 collective-permute-start.1
  154.8 30.3 %collective-permute-done.1 = bf16[2,16,16384]{2,1,0:T(8,128)(2,1)} collective-permute-done((bf16[2,16,16384]{2,1,0:T(8,128)(2,1)S(1)}, bf16[2,16,16384]{2,1,0:T(8,128)(2,1)}, u32[]{:S(2)}, u32[]{:S(2)}) %collective-permute-start.1) | collective-permute-done | bytes 1048608 | tf_op jit(solution)/shard_map/ppermute | solution.py:22
  186.5 16.0 %reduce-scatter.3.cloned.1.call-done = f32[16,16384]{1,0:T(8,128)} async-done(((f32[64,16384]{1,0:T(8,128)}), f32[16,16384]{1,0:T(8,128)}) %reduce-scatter.3.cloned.1.call-update) | async-done | bytes 1048592 | tf_op jit(solution)/shard_map/reduce_scatter | solution.py:50
  202.7 4.6 %fusion.1 = f32[8,64]{1,0:T(8,128)S(1)} fusion(bf16[24,8,16384]{2,0,1:T(8,128)(2,1)} %stack.3, bf16[64,16384,1]{1,0,2:T(8,128)(2,1)S(1)} %bitcast.80, s32[8,24,64]{2,1,0:T(8,128)S(1)} %copy-done.3, s32[8,64]{1,0:T(8,128)S(1)} %copy-done.2), kind=kOutput, calls=%fused_computation.4 | convolution fusion | flops 402701824 | bytes 8441856 | tf_op jit(solution)/shard_map/dot_general | solution.py:45
  208.0 63.3 %reduce-scatter.5.cloned.1.call-done = f32[16,2048]{1,0:T(8,128)} async-done(((f32[16,16384]{1,0:T(8,128)}), f32[16,2048]{1,0:T(8,128)}) %reduce-scatter.5.cloned.1.call-update) | async-done | bytes 131088 | tf_op jit(solution)/shard_map/reduce_scatter | solution.py:56
  (131 shorter events, 77.9 us)
Async XLA Ops:
  7.2 12.4 %copy-start = (bf16[8,16384]{1,0:T(8,128)(2,1)S(1)}, bf16[8,16384]{1,0:T(8,128)(2,1)}, u32[]{:S(2)}) copy-start(bf16[8,16384]{1,0:T(8,128)(2,1)} %param.4) | copy-start | bytes 786436
  7.2 195.3 %reduce-scatter.3.cloned.1.call-start = ((), (), s32[]{:S(2)}) async-start(), calls=%async_computation.2 | async-start | bytes 5242880 | tf_op jit(solution)/shard_map/reduce_scatter | solution.py:50
  7.2 143.0 %collective-permute-start = (bf16[1,16,16384]{2,1,0:T(8,128)(2,1)}, bf16[1,16,16384]{2,1,0:T(8,128)(2,1)}, u32[]{:S(2)}, u32[]{:S(2)}) collective-permute-start(bf16[1,16,16384]{2,1,0:T(8,128)(2,1)} %bitcast.81), channel_id=1, source_target_pairs={{0,1},{1,0},{2,3},{3,2},{4,5},{5,4},{6,7},{7,6},{8,9},{9,8},{10,11... | collective-permute-start | bytes 1572872 | tf_op jit(solution)/shard_map/ppermute | solution.py:22
  109.4 34.4 %copy-start.2 = (s32[8,64]{1,0:T(8,128)S(1)}, s32[8,64]{1,0:T(8,128)}, u32[]{:S(2)}) copy-start(s32[8,64]{1,0:T(8,128)} %param.7) | copy-start | bytes 6148
  109.4 34.4 %copy-start.3 = (s32[8,24,64]{2,1,0:T(8,128)S(1)}, s32[8,24,64]{2,1,0:T(8,128)}, u32[]{:S(2)}) copy-start(s32[8,24,64]{2,1,0:T(8,128)} %param.6) | copy-start | bytes 147460
  150.0 1.0 copy-start.1
  150.0 121.3 %reduce-scatter.5.cloned.1.call-start = ((), (), s32[]{:S(2)}) async-start(), calls=%async_computation.3 | async-start | bytes 1179648 | tf_op jit(solution)/shard_map/reduce_scatter | solution.py:56
  152.2 32.9 %collective-permute-start.1 = (bf16[2,16,16384]{2,1,0:T(8,128)(2,1)S(1)}, bf16[2,16,16384]{2,1,0:T(8,128)(2,1)}, u32[]{:S(2)}, u32[]{:S(2)}) collective-permute-start(bf16[2,16,16384]{2,1,0:T(8,128)(2,1)S(1)} %pad_maximum_fusion.1), channel_id=1, source_target_pairs={{0,2},{1,3},{2,0},{3,1},{4,6},{5,7},{6,4},{7,5},{8,10},{9,11},{10,... | collective-permute-start | bytes 3145736 | tf_op jit(solution)/shard_map/ppermute | solution.py:22
Sparse Core Ops, SparseCore 0:
  150.1 52.3 reduce-scatter.2
  206.3 64.9 reduce-scatter.4
